TPU v7x, 256 devices: a whole 4x4x8 slice. The times are simulated.
256 devices in a mesh: row: 32 (over z, y), col: 8 (over x, core).
Axes of the slice: x: 4, y: 4, z: 8, core: 2. Of those that a mesh axis runs over, the one named last changes fastest.
Arguments:
- factor: bfloat16 [28672, 28672], P('row', 'col'), as said below
- basis: bfloat16 [28672, 512], P('row'), may hold values from -6 to 6
Outputs:
- eigen_basis: float32 [28672, 512], P(('row', 'col'))
- middle_basis: bfloat16 [28672, 512], P('col')
Inputs may be any that keep to these rules, and one draw needn't show every extreme that they name: factor is exactly symmetric.
All inputs are finite; a program needn't handle non-finite values.
Results may differ from a plain program's by a relative error of at most 0.0029.
Values may be sent and summed in bfloat16 or wider, within the bound.
No kernel may reach another device: no remote copies, remote signals or barrier semaphores. Data moves between devices by JAX's collectives and lax.ppermute only.
A program may use at most 128 MiB of HBM per device.

v0:
```python
import math

import jax
import jax.numpy as jnp
from jax import lax
from jax.sharding import PartitionSpec as P

M = 28672


def gram_of(values):
    return jnp.dot(
        values.T, values, precision=lax.Precision.HIGHEST, preferred_element_type=jnp.float32
    )


def apply_inverse(values, gram):
    lower = jnp.linalg.cholesky(gram)
    width = gram.shape[0]
    inverse = lax.linalg.triangular_solve(
        lower, jnp.eye(width, dtype=jnp.float32), left_side=True, lower=True
    )
    return jnp.dot(
        values, inverse.T, precision=lax.Precision.HIGHEST, preferred_element_type=jnp.float32
    )


def shards(factor, basis):
    scale = math.sqrt(M)
    block = factor
    first = lax.psum_scatter(
        lax.dot_general(block, basis, (((0,), (0,)), ((), ())), preferred_element_type=jnp.float32),
        "row",
        scatter_dimension=0,
        tiled=True,
    )
    gram_one = lax.psum(gram_of(first), ("row", "col"))
    middle = (apply_inverse(first, gram_one) * scale).astype(jnp.bfloat16)
    column_basis = lax.all_gather(middle, "row", axis=0, tiled=True)
    block = factor
    second = lax.psum_scatter(
        jnp.dot(block, column_basis, preferred_element_type=jnp.float32),
        "col",
        scatter_dimension=0,
        tiled=True,
    )
    gram_two = lax.psum(gram_of(second), ("row", "col"))
    return (apply_inverse(second, gram_two) * scale, column_basis)


def solution(mesh):
    return jax.shard_map(
        shards,
        mesh=mesh,
        in_specs=(P("row", "col"), P("row", None)),
        out_specs=(P(("row", "col"), None), P("col", None)),
        check_vma=False,
    )
```

profile of v0, /device:TPU:1, one launch (start us, length us, event | category | flops | bytes accessed | tf_op | source)
XLA Modules:
  0.0 1210.3 jit_solution(10500507926553882362)
XLA Ops:
  8.3 9.0 fusion.80
  17.4 226.8 %reduce-scatter.5.cloned.1.call-done = f32[112,512]{1,0:T(8,128)} async-done(((f32[3584,512]{1,0:T(8,128)}), f32[112,512]{1,0:T(8,128)}) %reduce-scatter.5.cloned.1.call-update) | async-done | bytes 229392 | tf_op jit(solution)/shard_map/reduce_scatter | solution.py:31
  244.2 3.0 fusion.81
  247.7 260.1 %all-reduce.4.cloned.1.call-done = f32[512,512]{0,1:T(8,128)} async-done(((f32[512,512]{0,1:T(8,128)}), f32[512,512]{0,1:T(8,128)}) %all-reduce.4.cloned.1.call-update) | async-done | bytes 1048592 | tf_op jit(solution)/shard_map/psum | solution.py:37
  507.8 1.6 copy.9
  509.4 1.4 fusion.16
  511.8 11.7 cholesky.286
  523.6 9.8 custom-call.27
  536.7 12.5 %cholesky.305 = f32[128,128]{1,0:T(8,128)S(1)} custom-call(f32[128,128]{1,0:T(8,128)} %cholesky.430), custom_call_target="Cholesky" | custom-call | tf_op jit(solution)/shard_map/jit(cholesky)/cholesky | solution.py:18
  549.9 11.1 custom-call.28
  562.6 11.7 cholesky.326
  575.1 9.8 custom-call.29
  586.3 11.7 cholesky.343
  603.2 12.0 while.4
  603.9 2.3 bitcast_dynamic-update-slice_fusion.4
  606.9 2.3 bitcast_dynamic-update-slice_fusion.4
  609.9 2.3 bitcast_dynamic-update-slice_fusion.4
  613.0 2.3 bitcast_dynamic-update-slice_fusion.4
  615.2 39.3 %custom-call.30 = f32[4,128,128]{1,2,0:T(8,128)S(1)} custom-call(f32[4,128,128]{2,1,0:T(8,128)S(1)} %get-tuple-element.18), custom_call_target="InvertDiagBlocksLowerTriangular" | custom-call | tf_op jit(solution)/shard_map/triangular_solve/custom-call.3 | solution.py:20
  656.6 1.3 convolution_subtract_fusion.2
  658.4 1.6 convolution_subtract_fusion.5
  660.4 1.8 fusion
  662.3 78.0 %all-gather.2.cloned.1.call-done = bf16[3584,512]{1,0:T(8,128)(2,1)} async-done(((bf16[112,512]{1,0:T(8,128)(2,1)}), bf16[3584,512]{1,0:T(8,128)(2,1)}) %all-gather.2.cloned.1.call-update) | async-done | bytes 3670032 | tf_op jit(solution)/shard_map/all_gather | solution.py:39
  740.3 9.2 convolution_bitcast_fusion
  749.4 2.8 copy.14
  752.5 33.1 %reduce-scatter.7.cloned.1.call-done = f32[112,512]{1,0:T(8,128)} async-done(((f32[896,512]{1,0:T(8,128)}), f32[112,512]{1,0:T(8,128)}) %reduce-scatter.7.cloned.1.call-update) | async-done | bytes 229392
  785.6 3.0 fusion.82
  788.7 258.6 %all-reduce.6.cloned.1.call-done = f32[512,512]{0,1:T(8,128)} async-done(((f32[512,512]{0,1:T(8,128)}), f32[512,512]{0,1:T(8,128)}) %all-reduce.6.cloned.1.call-update) | async-done | bytes 1048592 | tf_op jit(solution)/shard_map/psum | solution.py:47
  1047.3 1.6 copy.11
  1048.9 1.4 fusion.15
  1051.3 11.7 cholesky.358
  1063.2 9.8 custom-call.31
  1075.6 12.3 %cholesky.377 = f32[128,128]{1,0:T(8,128)} custom-call(f32[128,128]{1,0:T(8,128)S(1)} %cholesky.443), custom_call_target="Cholesky" | custom-call | tf_op jit(solution)/shard_map/jit(cholesky)/cholesky | solution.py:18
  1090.5 10.4 custom-call.32
  1103.4 11.7 cholesky.398
  1115.8 9.8 custom-call.33
  1127.0 11.9 cholesky.415
  1143.2 11.2 while.5
  1143.8 2.2 bitcast_dynamic-update-slice_fusion.5
  1146.7 2.2 bitcast_dynamic-update-slice_fusion.5
  1149.5 2.2 bitcast_dynamic-update-slice_fusion.5
  1152.3 2.1 bitcast_dynamic-update-slice_fusion.5
  1154.4 39.3 %custom-call.34 = f32[4,128,128]{1,2,0:T(8,128)S(1)} custom-call(f32[4,128,128]{2,1,0:T(8,128)S(1)} %get-tuple-element.19), custom_call_target="InvertDiagBlocksLowerTriangular" | custom-call | tf_op jit(solution)/shard_map/triangular_solve/custom-call.3 | solution.py:20
  1194.2 1.4 convolution_subtract_fusion.1
  1196.1 1.3 convolution_subtract_fusion
  1197.8 1.6 convolution_subtract_fusion.4
  1199.8 1.9 convolution_multiply_fusion
  1201.7 1.8 copy.49
  (89 shorter events, 35.5 us)
Async XLA Ops:
  7.2 1.2 copy-start
  7.2 237.0 %reduce-scatter.5.cloned.1.call-start = ((), (), s32[]{:S(2)}) async-start(), calls=%async_computation.2 | async-start | bytes 7569408 | tf_op jit(solution)/shard_map/reduce_scatter | solution.py:31
  17.4 490.4 %all-reduce.4.cloned.1.call-start = ((), (), s32[]{:S(2)}) async-start(), calls=%async_computation.3 | async-start | bytes 2097152 | tf_op jit(solution)/shard_map/psum | solution.py:37
  247.3 493.0 %all-gather.2.cloned.1.call-start = ((), (), s32[]{:S(2)}) async-start(), calls=%async_computation.4 | async-start | bytes 3784704 | tf_op jit(solution)/shard_map/all_gather | solution.py:39
  510.8 1.0 copy-start.3
  533.5 126.9 %copy-start.4 = (f32[112,512]{1,0:T(8,128)S(1)}, f32[112,512]{1,0:T(8,128)}, u32[]{:S(2)}) copy-start(f32[112,512]{1,0:T(8,128)} %reduce-scatter.5.cloned.1.call-done) | copy-start | bytes 688132
  662.3 123.4 %reduce-scatter.7.cloned.1.call-start = ((), (), s32[]{:S(2)}) async-start(), calls=%async_computation.6 | async-start | bytes 2064384
  752.3 295.1 %all-reduce.6.cloned.1.call-start = ((), (), s32[]{:S(2)}) async-start(), calls=%async_computation.5 | async-start | bytes 2097152 | tf_op jit(solution)/shard_map/psum | solution.py:47
  1050.3 1.0 copy-start.2
  1063.2 136.6 %copy-start.5 = (f32[112,512]{1,0:T(8,128)S(1)}, f32[112,512]{1,0:T(8,128)}, u32[]{:S(2)}) copy-start(f32[112,512]{1,0:T(8,128)} %reduce-scatter.7.cloned.1.call-done) | copy-start | bytes 688132
  1193.8 7.9 copy-start.1
Sparse Core Ops, SparseCore 0:
  17.5 226.6 reduce-scatter.4
  251.1 256.7 all-reduce.3
  662.4 77.8 all-gather.1
  752.4 33.2 reduce-scatter.6
  791.5 255.7 all-reduce.5
where the time goes:
time: 1220 us; the launch traced here: 1210 us
  waiting for transfers between devices  857 us (70%)
  other arithmetic  247 us (20%)
  matrix products  51.5 us (4%)
  local copies, waits for them, and re-layouts  34.9 us (3%)
  between operations  19.5 us (2%)
    psum x1, waiting for transfers between devices, shards(): gram_one = lax.psum(gram_of(first), ('row', 'col'))  260 us
    psum x1, waiting for transfers between devices, shards(): gram_two = lax.psum(gram_of(second), ('row', 'col'))  259 us
    reduce_scatter x1, waiting for transfers between devices, shards(): lax.psum_scatter(lax.dot_general(block, basis, (((0,), (0,)), ((), ())),...  227 us
    another operation x29, other arithmetic, apply_inverse(): lower = jnp.linalg.cholesky(gram)  163 us
    another operation x5, other arithmetic, apply_inverse(): lax.linalg.triangular_solve(lower, jnp.eye(width, dtype=jnp.float32), lef...  80.8 us
    all_gather x1, waiting for transfers between devices, shards(): column_basis = lax.all_gather(middle, 'row', axis=0, tiled=True)  78 us
    unnamed x6, waiting for transfers between devices  33.2 us
  transfers between devices with their start and end apart: 5, of which 5 were waited for; matrix products, arithmetic and copies ran while one was open for 0% of the time, Pallas kernels for 0%

commit v1 on v0

v1 whole, which is shorter than its diff:
```python
import math

import jax
import jax.numpy as jnp
from jax import lax
from jax.experimental import pallas as pl
from jax.experimental.pallas import tpu as pltpu
from jax.sharding import PartitionSpec as P

M = 28672
K = 512
B = 128
R = 8


def dot(a, b, ca, cb):
    return lax.dot_general(a, b, (((ca,), (cb,)), ((), ())), precision=lax.Precision.HIGHEST,
                           preferred_element_type=jnp.float32)


def leaf(block):
    n = B // R
    w = [block[R * i:R * i + R, :] for i in range(n)]
    lane = lax.broadcasted_iota(jnp.int32, (R, B), 1)
    sub = lax.broadcasted_iota(jnp.int32, (R, B), 0)
    done = []
    for p in range(n):
        at = R * p
        top = w[p]
        inside = (lane >= at) & (lane < at + R)
        columns = [jnp.broadcast_to(top[:, at + j:at + j + 1], (R, B)) for j in range(R)]
        entry = {(i, j): jnp.broadcast_to(columns[j][i:i + 1, :], (R, B)) for i in range(R) for j in range(i + 1)}
        rhs = jnp.where(inside, jnp.where(lane - at == sub, 1.0, 0.0), top)
        row = [jnp.broadcast_to(rhs[i:i + 1, :], (R, B)) for i in range(R)]
        ratio = {}
        over = []
        for k in range(R):
            over.append(1.0 / entry[k, k])
            for i in range(k + 1, R):
                ratio[i, k] = entry[i, k] * over[k]
            for i in range(k + 1, R):
                for j in range(k + 1, i + 1):
                    entry[i, j] = entry[i, j] - ratio[i, k] * entry[j, k]
            for i in range(k + 1, R):
                row[i] = row[i] - ratio[i, k] * row[k]
        back = [None] * R
        for k in reversed(range(R)):
            z = row[k] * over[k]
            for i in range(k + 1, R):
                z = z - ratio[i, k] * back[i]
            back[k] = z
        out = row[0] * lax.rsqrt(entry[0, 0])
        for k in range(1, R):
            out = jnp.where(sub == k, row[k] * lax.rsqrt(entry[k, k]), out)
        done.append(jnp.where(lane < at + R, out, 0.0))
        for i in range(p + 1, n):
            new = jnp.where(inside, 0.0, w[i])
            for j in range(R):
                new = new - jnp.broadcast_to(w[i][:, at + j:at + j + 1], (R, B)) * back[j]
            w[i] = new
    return jnp.concatenate(done, axis=0)


def chol_inverse(gram_ref, out_ref, work):
    n = K // B
    work[...] = gram_ref[...]
    for b in range(n):
        at = B * b
        low = leaf(work[at:at + B, at:at + B])
        work[at:at + B, at:at + B] = jnp.where(
            lax.broadcasted_iota(jnp.int32, (B, B), 0) == lax.broadcasted_iota(jnp.int32, (B, B), 1), 1.0, 0.0)
        top = dot(low, work[at:at + B, :], 1, 0)
        out_ref[at:at + B, :] = jnp.where(lax.broadcasted_iota(jnp.int32, (B, K), 1) < at + B, top, 0.0)
        for i in range(b + 1, n):
            to = B * i
            work[to:to + B, at:at + B] = jnp.zeros((B, B), jnp.float32)
            work[to:to + B, :] = work[to:to + B, :] - dot(top[:, to:to + B], top, 0, 0)


def inverse_factor(gram):
    return pl.pallas_call(
        chol_inverse,
        out_shape=jax.ShapeDtypeStruct((K, K), jnp.float32),
        in_specs=[pl.BlockSpec(memory_space=pltpu.VMEM)],
        out_specs=pl.BlockSpec(memory_space=pltpu.VMEM),
        scratch_shapes=[pltpu.VMEM((K, K), jnp.float32)],
        compiler_params=pltpu.CompilerParams(vmem_limit_bytes=32 * 1024 * 1024),
        cost_estimate=pl.CostEstimate(flops=2 * K ** 3, bytes_accessed=8 * K * K, transcendentals=0),
    )(gram)


def summed_share(values, axis):
    size = lax.axis_size(axis)
    pieces = values.reshape(size, values.shape[0] // size, values.shape[1])
    return jnp.sum(lax.all_to_all(pieces, axis, 0, 0, tiled=True), axis=0)


def column_rows(rows):
    height, width = lax.axis_size("row"), lax.axis_size("col")
    pairs = [(j, (j % height) * width + j // height) for j in range(height * width)]
    moved = lax.ppermute(rows, ("row", "col"), pairs)
    return lax.all_gather(moved, "row", axis=0, tiled=True)


def gram_inverse(values):
    gram = dot(values, values, 0, 0)
    share = summed_share(summed_share(gram, "col"), "row")
    whole = lax.all_gather(lax.all_gather(share, "row", axis=0, tiled=True), "col", axis=0, tiled=True)
    return inverse_factor(whole)


def shards(factor, basis):
    scale = math.sqrt(M)
    part = basis.shape[0] // lax.axis_size("col")
    own = lax.dynamic_slice_in_dim(basis, lax.axis_index("col") * part, part, 0)
    first = summed_share(jnp.dot(factor, column_rows(own), preferred_element_type=jnp.float32), "col")
    middle = (dot(first, gram_inverse(first), 1, 1) * scale).astype(jnp.bfloat16)
    column_basis = column_rows(middle)
    second = summed_share(jnp.dot(factor, column_basis, preferred_element_type=jnp.float32), "col")
    return (dot(second, gram_inverse(second), 1, 1) * scale, column_basis)


def solution(mesh):
    return jax.shard_map(
        shards,
        mesh=mesh,
        in_specs=(P("row", "col"), P("row", None)),
        out_specs=(P(("row", "col"), None), P("col", None)),
        check_vma=False,
    )
```

time: 1220 us -> 570 us (0.47)
  waiting for transfers between devices: 857 us -> 253 us
  other arithmetic: 247 us -> 3.65 us
  blocking collectives: 0 us -> 192 us
  Pallas kernels: 0 us -> 55.6 us
  matrix products: 51.5 us -> 23.3 us
  local copies, waits for them, and re-layouts: 34.9 us -> 14.5 us
    psum x2 -> x0, waiting for transfers between devices: 519 us -> none  [the longest x1 260 us: shards(): gram_one = lax.psum(gram_of(first), ('row', 'col'))]
    another operation x34 -> x0, other arithmetic: 244 us -> none  [the longest x29 163 us: apply_inverse(): lower = jnp.linalg.cholesky(gram)]
    reduce_scatter x1 -> x0, waiting for transfers between devices: 227 us -> none  [shards(): lax.psum_scatter(lax.dot_general(block, basis, (((0,), (0,)), ((), ())),...]
    all_gather x1 -> x4, waiting for transfers between devices: 78 us -> 235 us  [the longest x2 171 us: column_rows(): return lax.all_gather(moved, 'row', axis=0, tiled=True)]
    all_to_all x0 -> x6, blocking collectives: none -> 129 us  [summed_share(): return jnp.sum(lax.all_to_all(pieces, axis, 0, 0, tiled=True), axis=0)]
    all_gather x0 -> x2, blocking collectives: none -> 63.3 us  [gram_inverse(): lax.all_gather(share, 'row', axis=0, tiled=True)]
    pallas_call x0 -> x2, Pallas kernels: none -> 55.6 us  [inverse_factor(): pl.pallas_call(chol_inverse, out_shape=jax.ShapeDtypeStruct((K, K), jnp.f...]
    unnamed x6 -> x4, waiting for transfers between devices: 33.2 us -> 0.07 us
  transfers between devices with their start and end apart: 5 -> 6, of which waited for: 5 -> 6; matrix products, arithmetic and copies ran while one was open for 0% -> 0% of each run, Pallas kernels for 0% -> 0%
where the time goes in v1:
time: 570 us; the launch traced here: 564 us
  waiting for transfers between devices  253 us (44%)
  blocking collectives  192 us (34%)
  Pallas kernels  55.6 us (10%)
  matrix products  23.3 us (4%)
  local copies, waits for them, and re-layouts  14.5 us (3%)
  between operations  14.1 us (2%)
  starting transfers between devices  8.29 us (1%)
    all_gather x2, waiting for transfers between devices, column_rows(): return lax.all_gather(moved, 'row', axis=0, tiled=True)  171 us
    all_to_all x6, blocking collectives, summed_share(): return jnp.sum(lax.all_to_all(pieces, axis, 0, 0, tiled=True), axis=0)  129 us
    all_gather x2, waiting for transfers between devices, gram_inverse(): lax.all_gather(lax.all_gather(share, 'row', axis=0, tiled=True), 'col', a...  64.7 us
    all_gather x2, blocking collectives, gram_inverse(): lax.all_gather(share, 'row', axis=0, tiled=True)  63.3 us
    pallas_call x2, Pallas kernels, inverse_factor(): pl.pallas_call(chol_inverse, out_shape=jax.ShapeDtypeStruct((K, K), jnp.f...  55.6 us
    ppermute x2, waiting for transfers between devices, column_rows(): moved = lax.ppermute(rows, ('row', 'col'), pairs)  17.3 us
  transfers between devices with their start and end apart: 6, of which 6 were waited for; matrix products, arithmetic and copies ran while one was open for 0% of the time, Pallas kernels for 0%

profile of v1, /device:TPU:1, one launch (start us, length us, event | category | flops | bytes accessed | tf_op | source)
XLA Modules:
  0.0 564.3 jit_solution(10127398742081264765)
XLA Ops:
  7.2 0.0 all-gather.7.cloned.1.call-start
  7.2 1.1 copy-done
  8.4 4.6 collective-permute-start
  13.0 8.5 %collective-permute-done = bf16[112,512]{1,0:T(8,128)(2,1)S(1)} collective-permute-done((bf16[112,512]{1,0:T(8,128)(2,1)S(1)}, bf16[112,512]{1,0:T(8,128)(2,1)S(1)}, u32[]{:S(2)}, u32[]{:S(2)}) %collective-permute-start) | collective-permute-done | bytes 114720 | tf_op jit(solution)/shard_map/ppermute | solution.py:101
  21.5 0.6 copy-done.3
  22.2 0.0 all-gather.9.cloned.1.call-start
  22.2 86.9 %all-gather.7.cloned.1.call-done = bf16[3584,512]{1,0:T(8,128)(2,1)} async-done(((bf16[112,512]{1,0:T(8,128)(2,1)}), bf16[3584,512]{1,0:T(8,128)(2,1)}) %all-gather.7.cloned.1.call-update) | async-done | bytes 3670032 | tf_op jit(solution)/shard_map/all_gather | solution.py:102
  109.1 9.2 %convolution_bitcast_fusion.1 = f32[896,512]{0,1:T(8,128)} fusion(bf16[3584,512]{1,0:T(8,128)(2,1)} %all-gather.7.cloned.1.call-done, bf16[896,3584]{1,0:T(8,128)(2,1)} %param.2), kind=kOutput, calls=%fused_computation.1 | convolution fusion | flops 3288334336 | bytes 11927552 | tf_op jit(solution)/shard_map/dot_general | solution.py:116
  118.2 1.8 copy.18
  120.1 31.7 %all_to_all.30 = f32[8,112,512]{2,1,0:T(8,128)} all-to-all(f32[8,112,512]{2,1,0:T(8,128)S(1)} %bitcast.28), channel_id=1, replica_groups=mesh['row'=32,'col'=8] {'col'}, dimensions={0} | all-to-all | bytes 3670016 | tf_op jit(solution)/shard_map/all_to_all | solution.py:95
  151.8 1.7 reduce_sum.54
  153.5 0.1 copy.19
  153.6 1.0 fusion.3
  154.6 18.5 %all_to_all.31 = f32[8,64,512]{2,1,0:T(8,128)S(1)} all-to-all(f32[8,64,512]{2,1,0:T(8,128)S(1)} %fusion.3), channel_id=1, replica_groups=mesh['row'=32,'col'=8] {'col'}, dimensions={0} | all-to-all | bytes 2097152 | tf_op jit(solution)/shard_map/all_to_all | solution.py:95
  173.1 0.1 reduce_sum.55
  173.2 0.1 reshape.21
  173.3 14.2 %all_to_all.32 = f32[32,2,512]{2,1,0:T(2,128)S(1)} all-to-all(f32[32,2,512]{2,1,0:T(2,128)S(1)} %reshape.21), channel_id=1, replica_groups=mesh['row'=32,'col'=8] {'row'}, dimensions={0} | all-to-all | bytes 262144 | tf_op jit(solution)/shard_map/all_to_all | solution.py:95
  187.5 0.1 reduce_sum.56
  187.6 31.6 %all-gather = f32[32,2,512]{2,1,0:T(2,128)S(1)} all-gather(f32[1,2,512]{2,1,0:T(2,128)S(1)} %bitcast.35), channel_id=1, replica_groups=mesh['row'=32,'col'=8] {'row'}, dimensions={0}, use_global_device_ids=true | all-gather | bytes 135168 | tf_op jit(solution)/shard_map/all_gather | solution.py:108
  219.1 0.7 reshape.25
  219.9 0.3 all-gather.11.cloned.1.call-start
  220.3 32.2 %all-gather.9.cloned.1.call-done.gram_ref = f32[512,512]{1,0:T(8,128)} async-done(((f32[64,512]{1,0:T(8,128)}), f32[512,512]{1,0:T(8,128)}) %all-gather.9.cloned.1.call-update) | async-done | bytes 1048592 | tf_op jit(solution)/shard_map/all_gather | solution.py:108
  252.5 1.2 copy-done.1
  253.7 27.9 %shard_map.41 = f32[512,512]{1,0:T(8,128)S(1)} custom-call(f32[512,512]{1,0:T(8,128)S(1)} %copy-done.1), custom_call_target="tpu_custom_call" | custom-call | flops 268435456 | bytes 2097152 | tf_op jit(solution)/shard_map/pallas_call | solution.py:81
  281.6 1.2 fusion
  282.8 3.2 collective-permute-start.1
  286.1 8.7 %collective-permute-done.1 = bf16[112,512]{1,0:T(8,128)(2,1)S(1)} collective-permute-done((bf16[112,512]{1,0:T(8,128)(2,1)S(1)}, bf16[112,512]{1,0:T(8,128)(2,1)S(1)}, u32[]{:S(2)}, u32[]{:S(2)}) %collective-permute-start.1) | collective-permute-done | bytes 114720 | tf_op jit(solution)/shard_map/ppermute | solution.py:101
  294.8 0.6 copy-done.4
  295.5 0.0 all-gather.13.cloned.1.call-start
  295.5 83.6 %all-gather.11.cloned.1.call-done = bf16[3584,512]{1,0:T(8,128)(2,1)} async-done(((bf16[112,512]{1,0:T(8,128)(2,1)}), bf16[3584,512]{1,0:T(8,128)(2,1)}) %all-gather.11.cloned.1.call-update) | async-done | bytes 3670032 | tf_op jit(solution)/shard_map/all_gather | solution.py:102
  379.2 9.2 %convolution_bitcast_fusion = f32[896,512]{0,1:T(8,128)} fusion(bf16[3584,512]{1,0:T(8,128)(2,1)} %all-gather.11.cloned.1.call-done, bf16[896,3584]{1,0:T(8,128)(2,1)} %param.2), kind=kOutput, calls=%fused_computation | convolution fusion | flops 3288334336 | bytes 11927552 | tf_op jit(solution)/shard_map/dot_general | solution.py:119
  388.3 1.8 copy.21
  390.1 31.7 %all_to_all.33 = f32[8,112,512]{2,1,0:T(8,128)} all-to-all(f32[8,112,512]{2,1,0:T(8,128)S(1)} %bitcast.29), channel_id=1, replica_groups=mesh['row'=32,'col'=8] {'col'}, dimensions={0} | all-to-all | bytes 3670016 | tf_op jit(solution)/shard_map/all_to_all | solution.py:95
  421.8 1.7 reduce_sum.57
  423.5 0.1 copy.22
  423.7 1.0 fusion.1
  424.6 18.5 %all_to_all.34 = f32[8,64,512]{2,1,0:T(8,128)S(1)} all-to-all(f32[8,64,512]{2,1,0:T(8,128)S(1)} %fusion.1), channel_id=1, replica_groups=mesh['row'=32,'col'=8] {'col'}, dimensions={0} | all-to-all | bytes 2097152 | tf_op jit(solution)/shard_map/all_to_all | solution.py:95
  443.2 0.1 reduce_sum.58
  443.2 0.1 reshape.23
  443.3 14.2 %all_to_all.35 = f32[32,2,512]{2,1,0:T(2,128)S(1)} all-to-all(f32[32,2,512]{2,1,0:T(2,128)S(1)} %reshape.23), channel_id=1, replica_groups=mesh['row'=32,'col'=8] {'row'}, dimensions={0} | all-to-all | bytes 262144 | tf_op jit(solution)/shard_map/all_to_all | solution.py:95
  457.6 0.1 reduce_sum.59
  457.6 31.8 %all-gather.1 = f32[32,2,512]{2,1,0:T(2,128)S(1)} all-gather(f32[1,2,512]{2,1,0:T(2,128)S(1)} %bitcast.34), channel_id=1, replica_groups=mesh['row'=32,'col'=8] {'row'}, dimensions={0}, use_global_device_ids=true | all-gather | bytes 135168 | tf_op jit(solution)/shard_map/all_gather | solution.py:108
  489.4 0.7 reshape.27
  490.2 32.5 %all-gather.13.cloned.1.call-done.gram_ref = f32[512,512]{1,0:T(8,128)} async-done(((f32[64,512]{1,0:T(8,128)}), f32[512,512]{1,0:T(8,128)}) %all-gather.13.cloned.1.call-update) | async-done | bytes 1048592 | tf_op jit(solution)/shard_map/all_gather | solution.py:108
  522.7 1.2 copy-done.2
  523.9 27.6 %shard_map.42 = f32[512,512]{1,0:T(8,128)S(1)} custom-call(f32[512,512]{1,0:T(8,128)S(1)} %copy-done.2), custom_call_target="tpu_custom_call" | custom-call | flops 268435456 | bytes 2097152 | tf_op jit(solution)/shard_map/pallas_call | solution.py:81
  551.5 1.9 convolution_multiply_fusion
  553.4 4.1 copy.27
  (10 shorter events, 0.1 us)
Async XLA Ops:
  7.2 1.2 copy-start
  7.2 101.9 %all-gather.7.cloned.1.call-start = ((), (), s32[]{:S(2)}) async-start(), calls=%async_computation.6 | async-start | bytes 3784704 | tf_op jit(solution)/shard_map/all_gather | solution.py:102
  8.4 13.1 %collective-permute-start = (bf16[112,512]{1,0:T(8,128)(2,1)S(1)}, bf16[112,512]{1,0:T(8,128)(2,1)S(1)}, u32[]{:S(2)}, u32[]{:S(2)}) collective-permute-start(bf16[112,512]{1,0:T(8,128)(2,1)S(1)} %constant_dynamic-slice_fusion), channel_id=1, source_target_pairs={{0,0},{1,8},{2,16},{3,24},{4,32},{5,40},{6,48},{7,56},{8,64},{9,72... | collective-permute-start | bytes 344072 | tf_op jit(solution)/shard_map/ppermute | solution.py:101
  21.5 0.6 copy-start.3
  22.2 230.3 %all-gather.9.cloned.1.call-start = ((), (), s32[]{:S(2)}) async-start(), calls=%async_computation.7 | async-start | bytes 1179648 | tf_op jit(solution)/shard_map/all_gather | solution.py:108
  219.9 159.2 %all-gather.11.cloned.1.call-start = ((), (), s32[]{:S(2)}) async-start(), calls=%async_computation.8 | async-start | bytes 3784704 | tf_op jit(solution)/shard_map/all_gather | solution.py:102
  252.5 1.2 copy-start.1
  282.8 12.0 %collective-permute-start.1 = (bf16[112,512]{1,0:T(8,128)(2,1)S(1)}, bf16[112,512]{1,0:T(8,128)(2,1)S(1)}, u32[]{:S(2)}, u32[]{:S(2)}) collective-permute-start(bf16[112,512]{1,0:T(8,128)(2,1)S(1)} %fusion), channel_id=1, source_target_pairs={{0,0},{1,8},{2,16},{3,24},{4,32},{5,40},{6,48},{7,56},{8,64},{9,72... | collective-permute-start | bytes 344072 | tf_op jit(solution)/shard_map/ppermute | solution.py:101
  294.8 0.6 copy-start.4
  295.5 227.2 %all-gather.13.cloned.1.call-start = ((), (), s32[]{:S(2)}) async-start(), calls=%async_computation.9 | async-start | bytes 1179648 | tf_op jit(solution)/shard_map/all_gather | solution.py:108
  522.7 1.2 copy-start.2
Sparse Core Ops, SparseCore 0:
  22.3 86.7 all-gather.6
  220.0 32.3 all-gather.8
  295.6 83.5 all-gather.10
  490.3 32.3 all-gather.12
